TPU v7x, 512 devices: a whole 4x4x16 slice. The times are simulated.
512 devices in a mesh: strip: 128 (over x, z, core), head: 4 (over y).
Axes of the slice: x: 4, y: 4, z: 16, core: 2. Of those that a mesh axis runs over, the one named last changes fastest.
Arguments:
- queries: bfloat16 [32768, 1024], P('strip', 'head'), may hold values from -40 to 40
- keys_in: bfloat16 [32768, 1024], P('strip', 'head'), may hold values from -40 to 40
- values_in: bfloat16 [32768, 1024], P('strip', 'head'), may hold values from -6 to 6
- grad_output: bfloat16 [32768, 1024], P('strip', 'head'), may hold values from -6 to 6
- w_output: bfloat16 [1024, 1024], P('head'), may hold values from -0.1875 to 0.1875
- link_dilation_index: int32 [256, 4], P('strip'), may hold values from 0 to 5, all different within a row
- clouds: int32 [256], P('strip'), may hold values 0 or 1
- edge_lengths: int32 [256], P('strip'), may hold values from 16 to 128
Outputs:
- attention_result: bfloat16 [32768, 1024], P('strip', 'head')
- grad_queries: bfloat16 [32768, 1024], P('strip', 'head')
- grad_keys: bfloat16 [32768, 1024], P('strip', 'head')
- grad_values: bfloat16 [32768, 1024], P('strip', 'head')
- grad_weight: float32 [1024, 1024], P('head')
Inputs may be any that keep to these rules, and one draw needn't show every extreme that they name: `link_dilation_index`: each row names 4 different dilation steps.
All inputs are finite; a program needn't handle non-finite values. No bound on the sum of `clouds` on one device may be relied on, other than what follows from the above.
Results may differ from a plain program's by a relative error of at most 0.035.
Values may be sent and summed in bfloat16 or wider, within the bound.
A program may use at most 64 MiB of HBM per device.

v0:
```python
import jax
import jax.numpy as jnp
from jax import lax
from jax.sharding import PartitionSpec as P

HEAD_DIM = 64
BLOCK = 128
STEP_COUNT = 3


def shifted(value, axis, by):
    length = lax.axis_size(axis)
    pairs = [(i, i + by) for i in range(length) if 0 <= i + by < length]
    return lax.ppermute(value, axis, pairs)


def on_device(
    queries, keys_in, values_in, grad_output, w_output, link_dilation_index, clouds, edge_lengths
):
    groups = link_dilation_index.shape[0]
    link_count = link_dilation_index.shape[1]
    features = queries.shape[1]
    heads_here = features // HEAD_DIM
    score_scale = HEAD_DIM ** (-0.5)
    strips = lax.axis_size("strip")
    dilation = strips // 8
    slot_count = groups + link_count
    position = lax.broadcasted_iota(jnp.int32, (groups, BLOCK), 1)
    length_ok = position < edge_lengths[:, None]
    clear_sky = clouds == 0
    live_here = (length_ok & clear_sky[:, None]).astype(jnp.bfloat16)
    key_tiles = keys_in.reshape(groups, BLOCK, features)
    value_tiles = values_in.reshape(groups, BLOCK, features)
    bundle = (key_tiles, value_tiles, live_here)
    fetched = []
    for slot_index in range(2 * STEP_COUNT):
        strip_offset = (
            dilation * (slot_index + 1)
            if slot_index < STEP_COUNT
            else -dilation * (slot_index - STEP_COUNT + 1)
        )
        fetched.append(shifted((bundle[0], bundle[1], bundle[2]), "strip", -strip_offset))
    far_keys = jnp.stack([piece[0] for piece in fetched])
    distant_value_rows = jnp.stack([piece[1] for piece in fetched])
    far_live = jnp.stack([piece[2] for piece in fetched])
    group_ids = jnp.arange(groups)[:, None]
    near_keys = jnp.broadcast_to(key_tiles[None], (groups, groups, BLOCK, features))
    near_values = jnp.broadcast_to(value_tiles[None], (groups, groups, BLOCK, features))
    all_keys = jnp.concatenate([near_keys, far_keys[link_dilation_index, group_ids]], axis=1)
    all_values = jnp.concatenate(
        [near_values, distant_value_rows[link_dilation_index, group_ids]], axis=1
    )
    own_block = jnp.eye(groups, dtype=bool)
    near_live = length_ok[None, :, :] & (clear_sky[None, :, None] | own_block[:, :, None])
    live_keys = jnp.concatenate([near_live, far_live[link_dilation_index, group_ids] > 0.5], axis=1)
    query_heads = queries.reshape(groups, BLOCK, heads_here, HEAD_DIM)
    key_heads = all_keys.reshape(groups, slot_count, BLOCK, heads_here, HEAD_DIM)
    value_heads = all_values.reshape(groups, slot_count, BLOCK, heads_here, HEAD_DIM)
    scores = (
        jnp.einsum("gqhe,gkthe->ghqkt", query_heads, key_heads, preferred_element_type=jnp.float32)
        * score_scale
    )
    scores = jnp.where(live_keys[:, None, None, :, :], scores, -1e30)
    row_max = jnp.max(scores, axis=(3, 4), keepdims=True)
    weights = jnp.exp(scores - row_max)
    attention = weights / jnp.sum(weights, axis=(3, 4), keepdims=True)
    attention_low = attention.astype(jnp.bfloat16)
    attn_heads = jnp.einsum(
        "ghqkt,gkthe->gqhe", attention_low, value_heads, preferred_element_type=jnp.float32
    ).astype(jnp.bfloat16)
    attn = attn_heads.reshape(groups * BLOCK, features)
    partial_out = jnp.dot(attn, w_output, preferred_element_type=jnp.float32)
    attention_result = lax.psum_scatter(
        partial_out, "head", scatter_dimension=1, tiled=True
    ).astype(jnp.bfloat16)
    upstream = lax.all_gather(grad_output, "head", axis=1, tiled=True)
    grad_attn = lax.dot_general(
        upstream, w_output, (((1,), (1,)), ((), ())), preferred_element_type=jnp.float32
    ).astype(jnp.bfloat16)
    total_tokens = groups * BLOCK * strips
    weight_term = lax.dot_general(
        attn, upstream, (((0,), (0,)), ((), ())), preferred_element_type=jnp.float32
    ) * total_tokens ** (-0.5)
    grad_weight = lax.psum(weight_term, "strip")
    grad_heads = grad_attn.reshape(groups, BLOCK, heads_here, HEAD_DIM)
    correction = jnp.sum(grad_heads.astype(jnp.float32) * attn_heads.astype(jnp.float32), axis=3)
    correction = jnp.transpose(correction, (0, 2, 1))[:, :, :, None, None]
    grad_probs = jnp.einsum(
        "gqhe,gkthe->ghqkt", grad_heads, value_heads, preferred_element_type=jnp.float32
    )
    grad_scores = (attention * (grad_probs - correction)).astype(jnp.bfloat16)
    grad_queries = (
        jnp.einsum("ghqkt,gkthe->gqhe", grad_scores, key_heads, preferred_element_type=jnp.float32)
        * score_scale
    ).astype(jnp.bfloat16)
    grad_queries = grad_queries.reshape(groups * BLOCK, features)
    key_terms = (
        jnp.einsum(
            "ghqkt,gqhe->gkthe", grad_scores, query_heads, preferred_element_type=jnp.float32
        )
        * score_scale
    )
    value_terms = jnp.einsum(
        "ghqkt,gqhe->gkthe", attention_low, grad_heads, preferred_element_type=jnp.float32
    )
    key_terms = key_terms.reshape(groups, slot_count, BLOCK, features)
    value_terms = value_terms.reshape(groups, slot_count, BLOCK, features)
    key_total = jnp.sum(key_terms[:, :groups], axis=0)
    value_total = jnp.sum(value_terms[:, :groups], axis=0)
    far_key_grads = []
    far_value_grads = []
    for slot_index in range(2 * STEP_COUNT):
        selector = (link_dilation_index == slot_index).astype(jnp.float32)[:, :, None, None]
        far_key_grads.append(jnp.sum(selector * key_terms[:, groups:], axis=1))
        far_value_grads.append(jnp.sum(selector * value_terms[:, groups:], axis=1))
    for slot_index in range(2 * STEP_COUNT):
        strip_offset = (
            dilation * (slot_index + 1)
            if slot_index < STEP_COUNT
            else -dilation * (slot_index - STEP_COUNT + 1)
        )
        returned = shifted(
            (far_key_grads[slot_index], far_value_grads[slot_index]), "strip", strip_offset
        )
        key_total = key_total + returned[0]
        value_total = value_total + returned[1]
    grad_keys = key_total.astype(jnp.bfloat16).reshape(groups * BLOCK, features)
    grad_values = value_total.astype(jnp.bfloat16).reshape(groups * BLOCK, features)
    return (attention_result, grad_queries, grad_keys, grad_values, grad_weight)


def solution(mesh):
    return jax.shard_map(
        on_device,
        mesh=mesh,
        in_specs=(
            P("strip", "head"),
            P("strip", "head"),
            P("strip", "head"),
            P("strip", "head"),
            P("head", None),
            P("strip", None),
            P("strip"),
            P("strip"),
        ),
        out_specs=(
            P("strip", "head"),
            P("strip", "head"),
            P("strip", "head"),
            P("strip", "head"),
            P("head", None),
        ),
        check_vma=False,
    )
```

profile of v0, /device:TPU:1, one launch (start us, length us, event | category | flops | bytes accessed | tf_op | source)
XLA Modules:
  0.0 650.2 jit_solution(18382107580580633761)
XLA Ops:
  10.8 1.3 collective-permute-start.7
  12.1 1.3 collective-permute-start.8
  13.4 16.9 %collective-permute-start.9 = (bf16[2,128]{1,0:T(2,128)(2,1)S(1)}, bf16[2,128]{1,0:T(2,128)(2,1)S(1)}, u32[]{:S(2)}, u32[]{:S(2)}) collective-permute-start(bf16[2,128]{1,0:T(2,128)(2,1)S(1)} %get-tuple-element.50), channel_id=1, source_target_pairs={{0,64},{4,68},{8,72},{12,76},{16,80},{20,84},{24,88},{28,92},{32,9... | collective-permute-start | bytes 1544 | tf_op jit(solution)/shard_map/ppermute | solution.py:14
  30.3 4.6 collective-permute-start.10
  36.9 11.2 %all_gather.3 = bf16[256,1024]{1,0:T(8,128)(2,1)S(1)} all-gather(bf16[256,256]{1,0:T(8,128)(2,1)} %param.11), channel_id=1, replica_groups=mesh['strip'=128,'head'=4] {'head'}, dimensions={1}, use_global_device_ids=true | all-gather | bytes 655360 | tf_op jit(solution)/shard_map/all_gather | solution.py:76
  53.0 14.3 %collective-permute-start.11 = (bf16[2,128]{1,0:T(2,128)(2,1)S(1)}, bf16[2,128]{1,0:T(2,128)(2,1)S(1)}, u32[]{:S(2)}, u32[]{:S(2)}) collective-permute-start(bf16[2,128]{1,0:T(2,128)(2,1)S(1)} %get-tuple-element.50), channel_id=1, source_target_pairs={{0,192},{4,196},{8,200},{12,204},{16,208},{20,212},{24,216},{28,22... | collective-permute-start | bytes 1544 | tf_op jit(solution)/shard_map/ppermute | solution.py:14
  71.2 12.7 %collective-permute-start.15 = (bf16[2,128,256]{2,1,0:T(8,128)(2,1)S(1)}, bf16[2,128,256]{2,1,0:T(8,128)(2,1)S(1)}, u32[]{:S(2)}, u32[]{:S(2)}) collective-permute-start(bf16[2,128,256]{2,1,0:T(8,128)(2,1)S(1)} %bitcast.138), channel_id=1, source_target_pairs={{0,64},{4,68},{8,72},{12,76},{16,80},{20,84},{24,88},{28,92},{32,9... | collective-permute-start | bytes 393224 | tf_op jit(solution)/shard_map/ppermute | solution.py:14
  84.0 4.6 collective-permute-start.16
  89.2 14.5 %collective-permute-start.17 = (bf16[2,128,256]{2,1,0:T(8,128)(2,1)S(1)}, bf16[2,128,256]{2,1,0:T(8,128)(2,1)S(1)}, u32[]{:S(2)}, u32[]{:S(2)}) collective-permute-start(bf16[2,128,256]{2,1,0:T(8,128)(2,1)S(1)} %bitcast.140), channel_id=1, source_target_pairs={{0,192},{4,196},{8,200},{12,204},{16,208},{20,212},{24,216},{28,22... | collective-permute-start | bytes 393224 | tf_op jit(solution)/shard_map/ppermute | solution.py:14
  107.7 13.4 %collective-permute-start.3 = (bf16[2,128,256]{2,1,0:T(8,128)(2,1)S(1)}, bf16[2,128,256]{2,1,0:T(8,128)(2,1)}, u32[]{:S(2)}, u32[]{:S(2)}) collective-permute-start(bf16[2,128,256]{2,1,0:T(8,128)(2,1)S(1)} %bitcast.145), channel_id=1, source_target_pairs={{0,64},{4,68},{8,72},{12,76},{16,80},{20,84},{24,88},{28,92},{32,9... | collective-permute-start | bytes 393224 | tf_op jit(solution)/shard_map/ppermute | solution.py:14
  121.1 4.6 collective-permute-start.4
  126.7 13.8 %collective-permute-start.5 = (bf16[2,128,256]{2,1,0:T(8,128)(2,1)S(1)}, bf16[2,128,256]{2,1,0:T(8,128)(2,1)S(1)}, u32[]{:S(2)}, u32[]{:S(2)}) collective-permute-start(bf16[2,128,256]{2,1,0:T(8,128)(2,1)S(1)} %bitcast.147), channel_id=1, source_target_pairs={{0,192},{4,196},{8,200},{12,204},{16,208},{20,212},{24,216},{28,22... | collective-permute-start | bytes 393224 | tf_op jit(solution)/shard_map/ppermute | solution.py:14
  143.7 1.9 bitcast_reduce_fusion
  146.7 1.8 multiply_reduce_fusion.12
  148.7 1.3 fusion.16
  150.1 3.7 multiply_convert_fusion
  156.8 1.7 multiply_bitcast_fusion
  158.7 1.5 convolution_bitcast_fusion
  161.6 2.3 multiply_reduce_fusion.11
  167.8 17.8 %collective-permute-start.20 = (f32[2,128,256]{1,2,0:T(8,128)}, f32[2,128,256]{1,2,0:T(8,128)}, u32[]{:S(2)}, u32[]{:S(2)}) collective-permute-start(f32[2,128,256]{1,2,0:T(8,128)} %get-tuple-element.33), channel_id=1, source_target_pairs={{0,192},{4,196},{8,200},{12,204},{16,208},{20,212},{24,216},{28,22... | collective-permute-start | bytes 786440 | tf_op jit(solution)/shard_map/ppermute | solution.py:14
  185.6 11.7 %collective-permute-start.19 = (f32[2,128,256]{1,2,0:T(8,128)}, f32[2,128,256]{1,2,0:T(8,128)}, u32[]{:S(2)}, u32[]{:S(2)}) collective-permute-start(f32[2,128,256]{1,2,0:T(8,128)} %get-tuple-element.32), channel_id=1, source_target_pairs={{0,128},{4,132},{8,136},{12,140},{16,144},{20,148},{24,152},{28,15... | collective-permute-start | bytes 786440 | tf_op jit(solution)/shard_map/ppermute | solution.py:14
  197.3 1.3 convolution_multiply_fusion
  198.6 5.8 collective-permute-start.18
  209.5 14.9 %collective-permute-start.26 = (f32[2,128,256]{1,2,0:T(8,128)S(1)}, f32[2,128,256]{1,2,0:T(8,128)S(1)}, u32[]{:S(2)}, u32[]{:S(2)}) collective-permute-start(f32[2,128,256]{1,2,0:T(8,128)S(1)} %get-tuple-element.40), channel_id=1, source_target_pairs={{0,192},{4,196},{8,200},{12,204},{16,208},{20,212},{24,216},{28,22... | collective-permute-start | bytes 786440 | tf_op jit(solution)/shard_map/ppermute | solution.py:14
  224.4 11.7 %collective-permute-start.25 = (f32[2,128,256]{1,2,0:T(8,128)S(1)}, f32[2,128,256]{1,2,0:T(8,128)S(1)}, u32[]{:S(2)}, u32[]{:S(2)}) collective-permute-start(f32[2,128,256]{1,2,0:T(8,128)S(1)} %get-tuple-element.41), channel_id=1, source_target_pairs={{0,128},{4,132},{8,136},{12,140},{16,144},{20,148},{24,152},{28,15... | collective-permute-start | bytes 786440 | tf_op jit(solution)/shard_map/ppermute | solution.py:14
  236.0 2.3 collective-permute-done.29
  239.1 5.6 collective-permute-start.24
  244.7 1.4 add_convert_fusion.1
  246.9 7.5 %collective-permute-done.24 = f32[2,128,256]{1,2,0:T(8,128)S(1)} collective-permute-done((f32[2,128,256]{1,2,0:T(8,128)S(1)}, f32[2,128,256]{1,2,0:T(8,128)S(1)}, u32[]{:S(2)}, u32[]{:S(2)}) %collective-permute-start.24) | collective-permute-done | bytes 262176 | tf_op jit(solution)/shard_map/ppermute | solution.py:14
  256.2 1.6 convert_element_type.61
  257.8 382.6 %all-reduce.2.cloned.1.call-done = f32[256,1024]{1,0:T(8,128)} async-done(((f32[256,1024]{1,0:T(8,128)}), f32[256,1024]{1,0:T(8,128)}) %all-reduce.2.cloned.1.call-update) | async-done | bytes 1048592 | tf_op jit(solution)/shard_map/psum | solution.py:84
  640.4 2.3 copy.189
  (133 shorter events, 40.0 us)
Async XLA Ops:
  8.0 248.1 %reduce-scatter.2.cloned.1.call-start = ((), (), s32[]{:S(2)}) async-start(), calls=%async_computation.1 | async-start | bytes 1310720 | tf_op jit(solution)/shard_map/reduce_scatter | solution.py:73
  9.5 43.4 %collective-permute-start.6 = (bf16[2,128]{1,0:T(2,128)(2,1)S(1)}, bf16[2,128]{1,0:T(2,128)(2,1)S(1)}, u32[]{:S(2)}, u32[]{:S(2)}) collective-permute-start(bf16[2,128]{1,0:T(2,128)(2,1)S(1)} %get-tuple-element.50), channel_id=1, source_target_pairs={{64,0},{68,4},{72,8},{76,12},{80,16},{84,20},{88,24},{92,28},{96,3... | collective-permute-start | bytes 1544 | tf_op jit(solution)/shard_map/ppermute | solution.py:14
  10.8 56.4 %collective-permute-start.7 = (bf16[2,128]{1,0:T(2,128)(2,1)S(1)}, bf16[2,128]{1,0:T(2,128)(2,1)S(1)}, u32[]{:S(2)}, u32[]{:S(2)}) collective-permute-start(bf16[2,128]{1,0:T(2,128)(2,1)S(1)} %get-tuple-element.50), channel_id=1, source_target_pairs={{128,0},{132,4},{136,8},{140,12},{144,16},{148,20},{152,24},{156,2... | collective-permute-start | bytes 1544 | tf_op jit(solution)/shard_map/ppermute | solution.py:14
  12.1 56.5 %collective-permute-start.8 = (bf16[2,128]{1,0:T(2,128)(2,1)S(1)}, bf16[2,128]{1,0:T(2,128)(2,1)S(1)}, u32[]{:S(2)}, u32[]{:S(2)}) collective-permute-start(bf16[2,128]{1,0:T(2,128)(2,1)S(1)} %get-tuple-element.50), channel_id=1, source_target_pairs={{192,0},{196,4},{200,8},{204,12},{208,16},{212,20},{216,24},{220,2... | collective-permute-start | bytes 1544 | tf_op jit(solution)/shard_map/ppermute | solution.py:14
  13.4 56.5 %collective-permute-start.9 = (bf16[2,128]{1,0:T(2,128)(2,1)S(1)}, bf16[2,128]{1,0:T(2,128)(2,1)S(1)}, u32[]{:S(2)}, u32[]{:S(2)}) collective-permute-start(bf16[2,128]{1,0:T(2,128)(2,1)S(1)} %get-tuple-element.50), channel_id=1, source_target_pairs={{0,64},{4,68},{8,72},{12,76},{16,80},{20,84},{24,88},{28,92},{32,9... | collective-permute-start | bytes 1544 | tf_op jit(solution)/shard_map/ppermute | solution.py:14
  30.3 40.9 %collective-permute-start.10 = (bf16[2,128]{1,0:T(2,128)(2,1)S(1)}, bf16[2,128]{1,0:T(2,128)(2,1)S(1)}, u32[]{:S(2)}, u32[]{:S(2)}) collective-permute-start(bf16[2,128]{1,0:T(2,128)(2,1)S(1)} %get-tuple-element.50), channel_id=1, source_target_pairs={{0,128},{4,132},{8,136},{12,140},{16,144},{20,148},{24,152},{28,15... | collective-permute-start | bytes 1544 | tf_op jit(solution)/shard_map/ppermute | solution.py:14
  53.0 31.0 %collective-permute-start.11 = (bf16[2,128]{1,0:T(2,128)(2,1)S(1)}, bf16[2,128]{1,0:T(2,128)(2,1)S(1)}, u32[]{:S(2)}, u32[]{:S(2)}) collective-permute-start(bf16[2,128]{1,0:T(2,128)(2,1)S(1)} %get-tuple-element.50), channel_id=1, source_target_pairs={{0,192},{4,196},{8,200},{12,204},{16,208},{20,212},{24,216},{28,22... | collective-permute-start | bytes 1544 | tf_op jit(solution)/shard_map/ppermute | solution.py:14
  67.3 22.0 %collective-permute-start.12 = (bf16[2,128,256]{2,1,0:T(8,128)(2,1)S(1)}, bf16[2,128,256]{2,1,0:T(8,128)(2,1)S(1)}, u32[]{:S(2)}, u32[]{:S(2)}) collective-permute-start(bf16[2,128,256]{2,1,0:T(8,128)(2,1)S(1)} %bitcast.135), channel_id=1, source_target_pairs={{64,0},{68,4},{72,8},{76,12},{80,16},{84,20},{88,24},{92,28},{96,3... | collective-permute-start | bytes 393224 | tf_op jit(solution)/shard_map/ppermute | solution.py:14
  68.6 35.2 %collective-permute-start.13 = (bf16[2,128,256]{2,1,0:T(8,128)(2,1)S(1)}, bf16[2,128,256]{2,1,0:T(8,128)(2,1)S(1)}, u32[]{:S(2)}, u32[]{:S(2)}) collective-permute-start(bf16[2,128,256]{2,1,0:T(8,128)(2,1)S(1)} %bitcast.136), channel_id=1, source_target_pairs={{128,0},{132,4},{136,8},{140,12},{144,16},{148,20},{152,24},{156,2... | collective-permute-start | bytes 393224 | tf_op jit(solution)/shard_map/ppermute | solution.py:14
  69.9 35.2 %collective-permute-start.14 = (bf16[2,128,256]{2,1,0:T(8,128)(2,1)S(1)}, bf16[2,128,256]{2,1,0:T(8,128)(2,1)S(1)}, u32[]{:S(2)}, u32[]{:S(2)}) collective-permute-start(bf16[2,128,256]{2,1,0:T(8,128)(2,1)S(1)} %bitcast.137), channel_id=1, source_target_pairs={{192,0},{196,4},{200,8},{204,12},{208,16},{212,20},{216,24},{220,2... | collective-permute-start | bytes 393224 | tf_op jit(solution)/shard_map/ppermute | solution.py:14
  71.2 35.2 %collective-permute-start.15 = (bf16[2,128,256]{2,1,0:T(8,128)(2,1)S(1)}, bf16[2,128,256]{2,1,0:T(8,128)(2,1)S(1)}, u32[]{:S(2)}, u32[]{:S(2)}) collective-permute-start(bf16[2,128,256]{2,1,0:T(8,128)(2,1)S(1)} %bitcast.138), channel_id=1, source_target_pairs={{0,64},{4,68},{8,72},{12,76},{16,80},{20,84},{24,88},{28,92},{32,9... | collective-permute-start | bytes 393224 | tf_op jit(solution)/shard_map/ppermute | solution.py:14
  84.0 23.8 %collective-permute-start.16 = (bf16[2,128,256]{2,1,0:T(8,128)(2,1)S(1)}, bf16[2,128,256]{2,1,0:T(8,128)(2,1)S(1)}, u32[]{:S(2)}, u32[]{:S(2)}) collective-permute-start(bf16[2,128,256]{2,1,0:T(8,128)(2,1)S(1)} %bitcast.139), channel_id=1, source_target_pairs={{0,128},{4,132},{8,136},{12,140},{16,144},{20,148},{24,152},{28,15... | collective-permute-start | bytes 393224 | tf_op jit(solution)/shard_map/ppermute | solution.py:14
  89.2 31.9 %collective-permute-start.17 = (bf16[2,128,256]{2,1,0:T(8,128)(2,1)S(1)}, bf16[2,128,256]{2,1,0:T(8,128)(2,1)S(1)}, u32[]{:S(2)}, u32[]{:S(2)}) collective-permute-start(bf16[2,128,256]{2,1,0:T(8,128)(2,1)S(1)} %bitcast.140), channel_id=1, source_target_pairs={{0,192},{4,196},{8,200},{12,204},{16,208},{20,212},{24,216},{28,22... | collective-permute-start | bytes 393224 | tf_op jit(solution)/shard_map/ppermute | solution.py:14
  103.8 22.9 %collective-permute-start = (bf16[2,128,256]{2,1,0:T(8,128)(2,1)S(1)}, bf16[2,128,256]{2,1,0:T(8,128)(2,1)S(1)}, u32[]{:S(2)}, u32[]{:S(2)}) collective-permute-start(bf16[2,128,256]{2,1,0:T(8,128)(2,1)S(1)} %bitcast.142), channel_id=1, source_target_pairs={{64,0},{68,4},{72,8},{76,12},{80,16},{84,20},{88,24},{92,28},{96,3... | collective-permute-start | bytes 393224 | tf_op jit(solution)/shard_map/ppermute | solution.py:14
  105.1 35.4 %collective-permute-start.1 = (bf16[2,128,256]{2,1,0:T(8,128)(2,1)S(1)}, bf16[2,128,256]{2,1,0:T(8,128)(2,1)S(1)}, u32[]{:S(2)}, u32[]{:S(2)}) collective-permute-start(bf16[2,128,256]{2,1,0:T(8,128)(2,1)S(1)} %bitcast.143), channel_id=1, source_target_pairs={{128,0},{132,4},{136,8},{140,12},{144,16},{148,20},{152,24},{156,2... | collective-permute-start | bytes 393224 | tf_op jit(solution)/shard_map/ppermute | solution.py:14
  106.4 34.1 %collective-permute-start.2 = (bf16[2,128,256]{2,1,0:T(8,128)(2,1)S(1)}, bf16[2,128,256]{2,1,0:T(8,128)(2,1)S(1)}, u32[]{:S(2)}, u32[]{:S(2)}) collective-permute-start(bf16[2,128,256]{2,1,0:T(8,128)(2,1)S(1)} %bitcast.144), channel_id=1, source_target_pairs={{192,0},{196,4},{200,8},{204,12},{208,16},{212,20},{216,24},{220,2... | collective-permute-start | bytes 393224 | tf_op jit(solution)/shard_map/ppermute | solution.py:14
  107.7 32.8 %collective-permute-start.3 = (bf16[2,128,256]{2,1,0:T(8,128)(2,1)S(1)}, bf16[2,128,256]{2,1,0:T(8,128)(2,1)}, u32[]{:S(2)}, u32[]{:S(2)}) collective-permute-start(bf16[2,128,256]{2,1,0:T(8,128)(2,1)S(1)} %bitcast.145), channel_id=1, source_target_pairs={{0,64},{4,68},{8,72},{12,76},{16,80},{20,84},{24,88},{28,92},{32,9... | collective-permute-start | bytes 393224 | tf_op jit(solution)/shard_map/ppermute | solution.py:14
  121.1 20.4 %collective-permute-start.4 = (bf16[2,128,256]{2,1,0:T(8,128)(2,1)S(1)}, bf16[2,128,256]{2,1,0:T(8,128)(2,1)}, u32[]{:S(2)}, u32[]{:S(2)}) collective-permute-start(bf16[2,128,256]{2,1,0:T(8,128)(2,1)S(1)} %bitcast.146), channel_id=1, source_target_pairs={{0,128},{4,132},{8,136},{12,140},{16,144},{20,148},{24,152},{28,15... | collective-permute-start | bytes 393224 | tf_op jit(solution)/shard_map/ppermute | solution.py:14
  126.7 16.1 %collective-permute-start.5 = (bf16[2,128,256]{2,1,0:T(8,128)(2,1)S(1)}, bf16[2,128,256]{2,1,0:T(8,128)(2,1)S(1)}, u32[]{:S(2)}, u32[]{:S(2)}) collective-permute-start(bf16[2,128,256]{2,1,0:T(8,128)(2,1)S(1)} %bitcast.147), channel_id=1, source_target_pairs={{0,192},{4,196},{8,200},{12,204},{16,208},{20,212},{24,216},{28,22... | collective-permute-start | bytes 393224 | tf_op jit(solution)/shard_map/ppermute | solution.py:14
  150.0 490.4 %all-reduce.2.cloned.1.call-start = ((), (), s32[]{:S(2)}) async-start(), calls=%async_computation.2 | async-start | bytes 2097152 | tf_op jit(solution)/shard_map/psum | solution.py:84
  163.9 34.7 %collective-permute-start.23 = (f32[2,128,256]{1,2,0:T(8,128)}, f32[2,128,256]{1,2,0:T(8,128)}, u32[]{:S(2)}, u32[]{:S(2)}) collective-permute-start(f32[2,128,256]{1,2,0:T(8,128)} %get-tuple-element.36), channel_id=1, source_target_pairs={{192,0},{196,4},{200,8},{204,12},{208,16},{212,20},{216,24},{220,2... | collective-permute-start | bytes 786440 | tf_op jit(solution)/shard_map/ppermute | solution.py:14
  165.2 39.2 %collective-permute-start.22 = (f32[2,128,256]{1,2,0:T(8,128)}, f32[2,128,256]{1,2,0:T(8,128)}, u32[]{:S(2)}, u32[]{:S(2)}) collective-permute-start(f32[2,128,256]{1,2,0:T(8,128)} %get-tuple-element.35), channel_id=1, source_target_pairs={{128,0},{132,4},{136,8},{140,12},{144,16},{148,20},{152,24},{156,2... | collective-permute-start | bytes 786440 | tf_op jit(solution)/shard_map/ppermute | solution.py:14
  166.5 40.3 %collective-permute-start.21 = (f32[2,128,256]{1,2,0:T(8,128)}, f32[2,128,256]{1,2,0:T(8,128)}, u32[]{:S(2)}, u32[]{:S(2)}) collective-permute-start(f32[2,128,256]{1,2,0:T(8,128)} %get-tuple-element.34), channel_id=1, source_target_pairs={{64,0},{68,4},{72,8},{76,12},{80,16},{84,20},{88,24},{92,28},{96,3... | collective-permute-start | bytes 786440 | tf_op jit(solution)/shard_map/ppermute | solution.py:14
  167.8 40.3 %collective-permute-start.20 = (f32[2,128,256]{1,2,0:T(8,128)}, f32[2,128,256]{1,2,0:T(8,128)}, u32[]{:S(2)}, u32[]{:S(2)}) collective-permute-start(f32[2,128,256]{1,2,0:T(8,128)} %get-tuple-element.33), channel_id=1, source_target_pairs={{0,192},{4,196},{8,200},{12,204},{16,208},{20,212},{24,216},{28,22... | collective-permute-start | bytes 786440 | tf_op jit(solution)/shard_map/ppermute | solution.py:14
  185.6 23.8 %collective-permute-start.19 = (f32[2,128,256]{1,2,0:T(8,128)}, f32[2,128,256]{1,2,0:T(8,128)}, u32[]{:S(2)}, u32[]{:S(2)}) collective-permute-start(f32[2,128,256]{1,2,0:T(8,128)} %get-tuple-element.32), channel_id=1, source_target_pairs={{0,128},{4,132},{8,136},{12,140},{16,144},{20,148},{24,152},{28,15... | collective-permute-start | bytes 786440 | tf_op jit(solution)/shard_map/ppermute | solution.py:14
  198.6 25.7 %collective-permute-start.18 = (f32[2,128,256]{1,2,0:T(8,128)}, f32[2,128,256]{1,2,0:T(8,128)S(1)}, u32[]{:S(2)}, u32[]{:S(2)}) collective-permute-start(f32[2,128,256]{1,2,0:T(8,128)} %get-tuple-element.31), channel_id=1, source_target_pairs={{0,64},{4,68},{8,72},{12,76},{16,80},{20,84},{24,88},{28,92},{32,9... | collective-permute-start | bytes 786440 | tf_op jit(solution)/shard_map/ppermute | solution.py:14
  204.4 34.0 %collective-permute-start.29 = (f32[2,128,256]{1,2,0:T(8,128)}, f32[2,128,256]{1,2,0:T(8,128)S(1)}, u32[]{:S(2)}, u32[]{:S(2)}) collective-permute-start(f32[2,128,256]{1,2,0:T(8,128)} %get-tuple-element.37), channel_id=1, source_target_pairs={{192,0},{196,4},{200,8},{204,12},{208,16},{212,20},{216,24},{220,2... | collective-permute-start | bytes 786440 | tf_op jit(solution)/shard_map/ppermute | solution.py:14
  206.8 40.0 %collective-permute-start.28 = (f32[2,128,256]{1,2,0:T(8,128)}, f32[2,128,256]{1,2,0:T(8,128)S(1)}, u32[]{:S(2)}, u32[]{:S(2)}) collective-permute-start(f32[2,128,256]{1,2,0:T(8,128)} %get-tuple-element.38), channel_id=1, source_target_pairs={{128,0},{132,4},{136,8},{140,12},{144,16},{148,20},{152,24},{156,2... | collective-permute-start | bytes 786440 | tf_op jit(solution)/shard_map/ppermute | solution.py:14
  208.2 38.7 %collective-permute-start.27 = (f32[2,128,256]{1,2,0:T(8,128)}, f32[2,128,256]{1,2,0:T(8,128)S(1)}, u32[]{:S(2)}, u32[]{:S(2)}) collective-permute-start(f32[2,128,256]{1,2,0:T(8,128)} %get-tuple-element.39), channel_id=1, source_target_pairs={{64,0},{68,4},{72,8},{76,12},{80,16},{84,20},{88,24},{92,28},{96,3... | collective-permute-start | bytes 786440 | tf_op jit(solution)/shard_map/ppermute | solution.py:14
  209.5 37.4 %collective-permute-start.26 = (f32[2,128,256]{1,2,0:T(8,128)S(1)}, f32[2,128,256]{1,2,0:T(8,128)S(1)}, u32[]{:S(2)}, u32[]{:S(2)}) collective-permute-start(f32[2,128,256]{1,2,0:T(8,128)S(1)} %get-tuple-element.40), channel_id=1, source_target_pairs={{0,192},{4,196},{8,200},{12,204},{16,208},{20,212},{24,216},{28,22... | collective-permute-start | bytes 786440 | tf_op jit(solution)/shard_map/ppermute | solution.py:14
  224.4 22.5 %collective-permute-start.25 = (f32[2,128,256]{1,2,0:T(8,128)S(1)}, f32[2,128,256]{1,2,0:T(8,128)S(1)}, u32[]{:S(2)}, u32[]{:S(2)}) collective-permute-start(f32[2,128,256]{1,2,0:T(8,128)S(1)} %get-tuple-element.41), channel_id=1, source_target_pairs={{0,128},{4,132},{8,136},{12,140},{16,144},{20,148},{24,152},{28,15... | collective-permute-start | bytes 786440 | tf_op jit(solution)/shard_map/ppermute | solution.py:14
  239.1 15.3 %collective-permute-start.24 = (f32[2,128,256]{1,2,0:T(8,128)S(1)}, f32[2,128,256]{1,2,0:T(8,128)S(1)}, u32[]{:S(2)}, u32[]{:S(2)}) collective-permute-start(f32[2,128,256]{1,2,0:T(8,128)S(1)} %get-tuple-element.42), channel_id=1, source_target_pairs={{0,64},{4,68},{8,72},{12,76},{16,80},{20,84},{24,88},{28,92},{32,9... | collective-permute-start | bytes 786440 | tf_op jit(solution)/shard_map/ppermute | solution.py:14
  (16 other events, 164.9 us)
Sparse Core Ops, SparseCore 0:
  150.1 55.5 reduce-scatter.1
Sparse Core Ops, SparseCore 1:
  198.7 441.7 all-reduce.1
where the time goes:
time: 651 us; the launch traced here: 650 us
  waiting for transfers between devices  393 us (60%)
  starting transfers between devices  186 us (29%)
  local copies, waits for them, and re-layouts  17 us (3%)
  between operations  16.3 us (3%)
  matrix products  14.6 us (2%)
  other arithmetic  11.9 us (2%)
  blocking collectives  11.2 us (2%)
    psum x1, waiting for transfers between devices, on_device(): grad_weight = lax.psum(weight_term, 'strip')  383 us
    ppermute x30, starting transfers between devices, shifted(): return lax.ppermute(value, axis, pairs)  186 us
  transfers between devices with their start and end apart: 32, of which 4 were waited for; matrix products, arithmetic and copies ran while one was open for 5% of the time, Pallas kernels for 0%

commit v1 on v0

v1 whole, which is shorter than its diff:
```python
import functools
import math

import jax
import jax.numpy as jnp
from jax import lax
from jax.experimental import pallas as pl
from jax.experimental.pallas import tpu as pltpu
from jax.sharding import PartitionSpec as P

HEAD_DIM = 64
BLOCK = 128
HEADS = 4
FEAT = 256
TOK = 256
SLOTS = 8
NEG = -1e30
F32 = jnp.float32
BF16 = jnp.bfloat16
SCALE = HEAD_DIM**-0.5
SCALE2 = SCALE * math.log2(math.e)
MESH = pl.DeviceIdType.MESH

STEPS = ((2, 2), (-2, -2), (1, -1), (3, 1), (-1, -3), (-3, 3))
SLOT_X = (1, -1, 0, 1, -1, 2)


def link_of(step):
    return step - 1 if step > 0 else 2 - step


def nt(a, b):
    return lax.dot_general(a, b, (((1,), (1,)), ((), ())), preferred_element_type=F32)


def nn(a, b):
    return jnp.dot(a, b, preferred_element_type=F32)


def kernel(
    tokens,
    q_ref,
    k_ref,
    v_ref,
    go_ref,
    w_ref,
    link_ref,
    cloud_ref,
    edge_ref,
    out_ref,
    dq_ref,
    dk_ref,
    dv_ref,
    dw_ref,
    kv,
    qg,
    meta,
    stat,
    dof,
    wc,
    at,
    qb,
    gb,
    bias,
    nkv,
    s_buf,
    p_buf,
    low_buf,
    mcol,
    rcol,
    dcol,
    dk_acc,
    dv_acc,
    dwp,
    cs,
    cr,
    xs,
    xr,
    zf,
    zs,
    zr,
    gx,
    gc,
    send,
    recv,
):
    strip = lax.axis_index("strip")
    y = lax.axis_index("head")
    core = strip % 2
    z = (strip // 2) % 16
    x = strip // 32
    upper = z // 8

    def at_chip(dx, dz, other=0):
        c = (core + other) % 2
        return (((x + dx + 4) % 4) * 32 + ((z + dz) % 16) * 2 + c, y)

    def at_head(dy):
        return (strip, (y + dy) % 4)

    counter = [0]

    def copy(src, dst, device):
        i = counter[0]
        counter[0] += 1
        made = pltpu.make_async_remote_copy(
            src_ref=src,
            dst_ref=dst,
            send_sem=send.at[i],
            recv_sem=recv.at[i],
            device_id=device,
            device_id_type=MESH,
        )
        return made

    for g in range(2):
        for b in range(2):
            rows = pl.ds(b * BLOCK, BLOCK)
            kv[0, g, 6 + b] = k_ref[rows, :]
            kv[1, g, 6 + b] = v_ref[rows, :]
            qg[0, g, 6 + b] = q_ref[rows, :]
    dof[y] = go_ref[...]
    wc[y] = w_ref[:, pl.ds(pl.multiple_of(y * FEAT, FEAT), FEAT)]

    row_id = lax.broadcasted_iota(jnp.int32, (16, BLOCK), 0)
    mine = jnp.zeros((16, BLOCK), jnp.int32)
    member = []
    for g in range(2):
        live = jnp.where(cloud_ref[g] == 0, edge_ref[g], 0)
        mine = jnp.where(row_id == g, live, mine)
        row = []
        for l in range(6):
            has = jnp.int32(0)
            for n in range(4):
                has = has + jnp.where(link_ref[g, n] == l, 1, 0)
            row.append(has)
            mine = jnp.where(row_id == 2 + 6 * g + l, has, mine)
        member.append(row)
    meta[6] = mine

    peers = [at_chip(0, dz) for dz in range(1, 16)]
    peers += [at_chip(dx, 0) for dx in (1, 2, 3)]
    peers += [at_chip(dx, 8) for dx in (1, 2, 3)]
    peers += [at_head(dy) for dy in (1, 2, 3)]
    peers += [at_chip(0, 0, 1)]
    barrier = pltpu.get_barrier_semaphore()
    for peer in peers:
        pl.semaphore_signal(barrier, inc=1, device_id=peer, device_id_type=MESH)
    pl.semaphore_wait(barrier, len(peers))

    z_kv = [copy(kv.at[:, g, 6 + g], kv.at[:, g, 2], at_chip(0, 8)) for g in range(2)]
    z_qg = [copy(qg.at[:, g, 6 + g], qg.at[:, g, 2], at_chip(0, 8)) for g in range(2)]

    def own_plane(buf, g):
        return [
            copy(buf.at[:, g, 6 + g], buf.at[:, g, 1], at_chip(1, 0)),
            copy(buf.at[:, g, 6 + g], buf.at[:, g, 0], at_chip(-1, 0)),
        ]

    def onward(buf, g):
        return [
            copy(buf.at[:, g, 2], buf.at[:, g, 4], at_chip(1, 0)),
            copy(buf.at[:, g, 2], buf.at[:, g, 3], at_chip(-1, 0)),
            copy(buf.at[:, g, 2], buf.at[:, g, 5], at_chip(2, 0)),
        ]

    def to_far(buf):
        return [
            copy(buf.at[6], buf.at[1], at_chip(1, 0)),
            copy(buf.at[6], buf.at[0], at_chip(-1, 0)),
            copy(buf.at[6], buf.at[2], at_chip(0, 8)),
            copy(buf.at[6], buf.at[4], at_chip(1, 8)),
            copy(buf.at[6], buf.at[3], at_chip(-1, 8)),
            copy(buf.at[6], buf.at[5], at_chip(2, 8)),
        ]

    x_kv = [own_plane(kv, g) for g in range(2)]
    x_qg = [own_plane(qg, g) for g in range(2)]
    f_kv = [onward(kv, g) for g in range(2)]
    f_qg = [onward(qg, g) for g in range(2)]
    meta_out = to_far(meta)
    stat_out = to_far(stat)
    y_go = [copy(dof.at[y], dof.at[y], at_head(dy)) for dy in (1, 2, 3)]
    y_w = [
        copy(
            w_ref.at[:, pl.ds(pl.multiple_of((y + dy) % 4 * FEAT, FEAT), FEAT)],
            wc.at[y],
            at_head(dy),
        )
        for dy in (1, 2, 3)
    ]
    y_at = [copy(at.at[y], at.at[y], at_head(dy)) for dy in (1, 2, 3)]
    c_rs = copy(cs, cr, at_chip(0, 0, 1))
    x_rs = [copy(xs.at[(x + dx) % 4], xr.at[dx], at_chip(dx, 0)) for dx in (1, 2, 3)]
    x_ag = [copy(gx.at[x], gx.at[x], at_chip(dx, 0)) for dx in (1, 2, 3)]
    c_ag = copy(gx, gc, at_chip(0, 0, 1))
    base = counter[0]

    def z_rs(dz):
        return pltpu.make_async_remote_copy(
            src_ref=zs.at[(z + dz) % 16],
            dst_ref=zr.at[dz],
            send_sem=send.at[base + dz],
            recv_sem=recv.at[base + dz],
            device_id=at_chip(0, dz),
            device_id_type=MESH,
        )

    def z_ag(dz):
        return pltpu.make_async_remote_copy(
            src_ref=gx.at[x, z],
            dst_ref=gx.at[x, z],
            send_sem=send.at[base + 16 + dz],
            recv_sem=recv.at[base + 16 + dz],
            device_id=at_chip(0, dz),
            device_id_type=MESH,
        )

    def start(copies):
        for made in copies:
            made.start()

    def arrived(copies):
        for made in copies:
            made.wait_recv()

    def sent(copies):
        for made in copies:
            made.wait_send()

    start(y_go)
    start(z_kv[:1])
    start(x_kv[0])
    start(z_kv[1:])
    start(x_kv[1])
    start(meta_out)
    start(y_w)

    head_of = lax.broadcasted_iota(jnp.int32, (1, FEAT), 1) // HEAD_DIM
    in_head = [jnp.where(head_of == h, 1.0, 0.0).astype(F32) for h in range(HEADS)]
    in_head_low = [m.astype(BF16) for m in in_head]

    def spread(block):
        return jnp.concatenate([block * m for m in in_head_low], axis=0)

    def gathered(full):
        total = full[:BLOCK] * in_head[0]
        for h in range(1, HEADS):
            total = total + full[h * BLOCK : (h + 1) * BLOCK] * in_head[h]
        return total

    for g in range(2):
        qb[g] = spread(q_ref[g * BLOCK : (g + 1) * BLOCK, :])

    arrived(y_go)
    grad = nt(dof[0], w_ref[:, :FEAT])
    for i in range(1, 4):
        grad = grad + nt(dof[i], w_ref[:, i * FEAT : (i + 1) * FEAT])
    grad = grad.astype(BF16)
    for g in range(2):
        for b in range(2):
            qg[1, g, 6 + b] = grad[b * BLOCK : (b + 1) * BLOCK]
        gb[g] = spread(grad[g * BLOCK : (g + 1) * BLOCK])
    start(x_qg[0])
    start(x_qg[1])

    arrived(z_kv[:1])
    start(f_kv[0])
    start(z_qg)
    arrived(z_kv[1:])
    start(f_kv[1])

    arrived(meta_out)
    lane = lax.broadcasted_iota(jnp.int32, (1, BLOCK), 1)
    chain = 2 * x + upper
    for g in range(2):
        own_live = jnp.where(cloud_ref[g] == 0, edge_ref[g], 0)
        for j in range(6):
            far = meta[j]
            low_step, high_step = STEPS[j]
            step = jnp.where(upper == 0, low_step, high_step)
            inside = jnp.where((chain + step >= 0) & (chain + step < 8), 1, 0)
            listed = inside * jnp.where(
                upper == 0, member[g][link_of(low_step)], member[g][link_of(high_step)]
            )
            live = far[g : g + 1] * listed
            bias[g, :, j * BLOCK : (j + 1) * BLOCK] = jnp.where(lane < live, 0.0, NEG).astype(F32)
            here_low = 2 + 6 * g + link_of(-low_step)
            here_high = 2 + 6 * g + link_of(-high_step)
            lists_us = jnp.where(
                upper == 0, far[here_low : here_low + 1], far[here_high : here_high + 1]
            )
            nkv[g, j] = lists_us * (inside * own_live)
        for b in range(2):
            live = edge_ref[b] if b == g else jnp.where(cloud_ref[b] == 0, edge_ref[b], 0)
            bias[g, :, (6 + b) * BLOCK : (7 + b) * BLOCK] = jnp.where(lane < live, 0.0, NEG).astype(F32)
            nkv[b, 6 + g] = jnp.full((1, BLOCK), live, jnp.int32)

    CHUNK = 32

    def forward(g):
        keys = kv[0, g].reshape(SLOTS * BLOCK, FEAT)
        s_buf[...] = nt(qb[g], keys)

        def soft(r, _):
            rows = pl.ds(pl.multiple_of(r * CHUNK, CHUNK), CHUNK)
            s = s_buf[rows, :] * SCALE2 + bias[g]
            top = jnp.max(s, axis=1, keepdims=True)
            e = jnp.exp2(s - top)
            inv = 1.0 / jnp.sum(e, axis=1, keepdims=True)
            p = e * inv
            p_buf[g, rows, :] = p
            low_buf[rows, :] = p.astype(BF16)
            mcol[g, rows, :] = jnp.broadcast_to(top, (CHUNK, BLOCK))
            rcol[g, rows, :] = jnp.broadcast_to(inv, (CHUNK, BLOCK))
            return 0

        lax.fori_loop(0, HEADS * BLOCK // CHUNK, soft, 0)
        full = nn(low_buf[...], kv[1, g].reshape(SLOTS * BLOCK, FEAT))
        at[y, g * BLOCK : (g + 1) * BLOCK, :] = gathered(full).astype(BF16)

    for g in range(2):
        arrived(x_kv[g])
        arrived(f_kv[g])
        forward(g)

    start(y_at)
    attn_t = at[y].astype(F32).T.astype(BF16)
    weight_scale = tokens ** (-0.5)
    for i in range(4):
        dwp[i] = nn(attn_t, dof[i]) * weight_scale
    theirs = pl.ds(pl.multiple_of((1 - core) * BLOCK, BLOCK), BLOCK)
    ours = pl.ds(pl.multiple_of(core * BLOCK, BLOCK), BLOCK)
    for i in range(4):
        cs[i] = dwp[i, theirs, :].astype(BF16)
    c_rs.start()

    lane_full = lax.broadcasted_iota(jnp.int32, (BLOCK, BLOCK), 1)

    def correction(g):
        t = qg[1, g, 6 + g].astype(F32) * at[y, g * BLOCK : (g + 1) * BLOCK, :].astype(F32)
        packed = jnp.zeros((BLOCK, BLOCK), F32)
        for h in range(HEADS):
            rows = slice(h * BLOCK, (h + 1) * BLOCK)
            d = jnp.broadcast_to(jnp.sum(t * in_head[h], axis=1, keepdims=True), (BLOCK, BLOCK))
            dcol[rows, :] = d
            packed = jnp.where(lane_full == h, mcol[g, rows, :], packed)
            packed = jnp.where(lane_full == HEADS + h, rcol[g, rows, :], packed)
            packed = jnp.where(lane_full == 2 * HEADS + h, d, packed)
        stat[6, g] = packed.T[:16]

    def backward_queries(g):
        keys = kv[0, g].reshape(SLOTS * BLOCK, FEAT)
        s_buf[...] = nt(gb[g], kv[1, g].reshape(SLOTS * BLOCK, FEAT))

        def body(r, _):
            rows = pl.ds(pl.multiple_of(r * CHUNK, CHUNK), CHUNK)
            ds = p_buf[g, rows, :] * (s_buf[rows, :] - dcol[rows, 0:1])
            low_buf[rows, :] = ds.astype(BF16)
            return 0

        lax.fori_loop(0, HEADS * BLOCK // CHUNK, body, 0)
        full = nn(low_buf[...], keys)
        dq_ref[g * BLOCK : (g + 1) * BLOCK, :] = (gathered(full) * SCALE).astype(BF16)

    row_full = lax.broadcasted_iota(jnp.int32, (BLOCK, BLOCK), 0)

    def keys_step(g, j, slot, group):
        key, value = kv[0, g, 6 + g], kv[1, g, 6 + g]
        query, cot = spread(qg[0, g, j]), spread(qg[1, g, j])
        st = nt(key, query)
        dp = nt(value, cot)
        off = jnp.where(row_full < nkv[g, j], 0.0, NEG).astype(F32)
        rows = stat[slot, group]
        lows, ds = [], []
        for h in range(HEADS):
            cols = slice(h * BLOCK, (h + 1) * BLOCK)
            top = rows[h : h + 1]
            inv = rows[HEADS + h : HEADS + h + 1]
            d = rows[2 * HEADS + h : 2 * HEADS + h + 1]
            p = jnp.exp2(st[:, cols] * SCALE2 + off - top) * inv
            lows.append(p.astype(BF16))
            ds.append((p * (dp[:, cols] - d)).astype(BF16))
        dv_acc[g] += nn(jnp.concatenate(lows, axis=1), cot)
        dk_acc[g] += nn(jnp.concatenate(ds, axis=1), query)

    def keys_near(g):
        dv_acc[g] = jnp.zeros((BLOCK, FEAT), F32)
        dk_acc[g] = jnp.zeros((BLOCK, FEAT), F32)

        def body(b, _):
            keys_step(g, 6 + b, 6, b)
            return 0

        lax.fori_loop(0, 2, body, 0)

    def keys_far(g, first, last):
        def body(j, _):
            keys_step(g, j, j, g)
            return 0

        lax.fori_loop(first, last, body, 0)

    arrived(z_qg[:1])
    start(f_qg[0])
    correction(0)
    backward_queries(0)

    c_rs.wait_recv()
    for i in range(4):
        xs[i] = (dwp[i, ours, :] + cr[i].astype(F32)).astype(BF16)
    start(x_rs)
    correction(1)
    start(stat_out)
    backward_queries(1)
    arrived(z_qg[1:])
    start(f_qg[1])

    arrived(x_rs)
    part = dwp[x, ours, :] + cr[x].astype(F32)
    for dx in (1, 2, 3):
        part = part + xr[dx].astype(F32)
    for i in range(16):
        piece = part[i // 2 * 16 : i // 2 * 16 + 16, i % 2 * 128 : i % 2 * 128 + 128]
        zf[i] = piece
        zs[i] = piece.astype(BF16)

    def each_z(act):
        def body(dz, _):
            act(dz)
            return 0

        lax.fori_loop(1, 16, body, 0)

    each_z(lambda dz: z_rs(dz).start())

    arrived(y_at)
    arrived(y_w)
    result = nn(at[0], wc[0])
    for i in range(1, 4):
        result = result + nn(at[i], wc[i])
    out_ref[...] = result.astype(BF16)

    for g in range(2):
        keys_near(g)

    each_z(lambda dz: z_rs(dz).wait_recv())
    total = zf[z]
    for dz in range(1, 16):
        total = total + zr[dz].astype(F32)
    gx[x, z] = total.astype(BF16)
    each_z(lambda dz: z_ag(dz).start())

    arrived(stat_out)
    for g in range(2):
        arrived(x_qg[g])
        keys_far(g, 0, 2)

    each_z(lambda dz: z_ag(dz).wait_recv())
    start(x_ag)
    arrived(f_qg[0])
    keys_far(0, 2, 6)
    arrived(x_ag)
    c_ag.start()
    arrived(f_qg[1])
    keys_far(1, 2, 6)
    for g in range(2):
        rows = slice(g * BLOCK, (g + 1) * BLOCK)
        dk_ref[rows, :] = (dk_acc[g] * SCALE).astype(BF16)
        dv_ref[rows, :] = dv_acc[g].astype(BF16)

    def assemble(buf, first_row):
        def body(i, _):
            for n in range(16):
                rows = pl.ds(pl.multiple_of(first_row + n // 2 * 16, 16), 16)
                cols = pl.ds(pl.multiple_of(i * FEAT + n % 2 * 128, 128), 128)
                dw_ref[rows, cols] = buf[i, n].astype(F32)
            return 0

        lax.fori_loop(0, 4, body, 0)

    assemble(gx, core * BLOCK)
    c_ag.wait_recv()
    assemble(gc, (1 - core) * BLOCK)

    for copies in (z_kv, z_qg, *x_kv, *x_qg, *f_kv, *f_qg, meta_out, stat_out, y_go, y_w, y_at):
        sent(copies)
    sent([c_rs, *x_rs, *x_ag, c_ag])
    each_z(lambda dz: z_rs(dz).wait_send())
    each_z(lambda dz: z_ag(dz).wait_send())


SEMAPHORES = 96


def on_device(
    queries, keys_in, values_in, grad_output, w_output, link_dilation_index, clouds, edge_lengths
):
    tokens = queries.shape[0] * lax.axis_size("strip")
    vmem = pl.BlockSpec(memory_space=pltpu.VMEM)
    smem = pl.BlockSpec(memory_space=pltpu.SMEM)
    block = jax.ShapeDtypeStruct((TOK, FEAT), BF16)
    return pl.pallas_call(
        functools.partial(kernel, tokens),
        out_shape=(block, block, block, block, jax.ShapeDtypeStruct((FEAT, 4 * FEAT), F32)),
        in_specs=[vmem] * 5 + [smem] * 3,
        out_specs=(vmem,) * 5,
        scratch_shapes=[
            pltpu.VMEM((2, 2, SLOTS, BLOCK, FEAT), BF16),
            pltpu.VMEM((2, 2, SLOTS, BLOCK, FEAT), BF16),
            pltpu.VMEM((7, 16, BLOCK), jnp.int32),
            pltpu.VMEM((7, 2, 16, BLOCK), F32),
            pltpu.VMEM((4, TOK, FEAT), BF16),
            pltpu.VMEM((4, FEAT, FEAT), BF16),
            pltpu.VMEM((4, TOK, FEAT), BF16),
            pltpu.VMEM((2, HEADS * BLOCK, FEAT), BF16),
            pltpu.VMEM((2, HEADS * BLOCK, FEAT), BF16),
            pltpu.VMEM((2, 1, SLOTS * BLOCK), F32),
            pltpu.VMEM((2, SLOTS, 1, BLOCK), jnp.int32),
            pltpu.VMEM((HEADS * BLOCK, SLOTS * BLOCK), F32),
            pltpu.VMEM((2, HEADS * BLOCK, SLOTS * BLOCK), F32),
            pltpu.VMEM((HEADS * BLOCK, SLOTS * BLOCK), BF16),
            pltpu.VMEM((2, HEADS * BLOCK, BLOCK), F32),
            pltpu.VMEM((2, HEADS * BLOCK, BLOCK), F32),
            pltpu.VMEM((HEADS * BLOCK, BLOCK), F32),
            pltpu.VMEM((2, BLOCK, FEAT), F32),
            pltpu.VMEM((2, BLOCK, FEAT), F32),
            pltpu.VMEM((4, FEAT, FEAT), F32),
            pltpu.VMEM((4, BLOCK, FEAT), BF16),
            pltpu.VMEM((4, BLOCK, FEAT), BF16),
            pltpu.VMEM((4, BLOCK, FEAT), BF16),
            pltpu.VMEM((4, BLOCK, FEAT), BF16),
            pltpu.VMEM((16, 16, 128), F32),
            pltpu.VMEM((16, 16, 128), BF16),
            pltpu.VMEM((16, 16, 128), BF16),
            pltpu.VMEM((4, 16, 16, 128), BF16),
            pltpu.VMEM((4, 16, 16, 128), BF16),
            pltpu.SemaphoreType.DMA((SEMAPHORES,)),
            pltpu.SemaphoreType.DMA((SEMAPHORES,)),
        ],
        compiler_params=pltpu.CompilerParams(
            collective_id=0, has_side_effects=True, vmem_limit_bytes=48 * 2**20
        ),
    )(queries, keys_in, values_in, grad_output, w_output, link_dilation_index, clouds, edge_lengths)


def solution(mesh):
    return jax.shard_map(
        on_device,
        mesh=mesh,
        in_specs=(
            P("strip", "head"),
            P("strip", "head"),
            P("strip", "head"),
            P("strip", "head"),
            P("head", None),
            P("strip", None),
            P("strip"),
            P("strip"),
        ),
        out_specs=(
            P("strip", "head"),
            P("strip", "head"),
            P("strip", "head"),
            P("strip", "head"),
            P("head", None),
        ),
        check_vma=False,
    )
```

time: 651 us -> 122 us (0.19)
  waiting for transfers between devices: 393 us -> 0 us
  starting transfers between devices: 186 us -> 0 us
  Pallas kernels: 0 us -> 111 us
  between operations: 16.3 us -> 0.66 us
  matrix products: 14.6 us -> 0 us
  other arithmetic: 11.9 us -> 0 us
  blocking collectives: 11.2 us -> 0 us
  local copies, waits for them, and re-layouts: 17 us -> 10.2 us
    psum x1 -> x0, waiting for transfers between devices: 383 us -> none  [on_device(): grad_weight = lax.psum(weight_term, 'strip')]
    ppermute x30 -> x0, starting transfers between devices: 186 us -> none  [shifted(): return lax.ppermute(value, axis, pairs)]
    pallas_call x0 -> x1, Pallas kernels: none -> 111 us  [on_device(): pl.pallas_call(functools.partial(kernel, tokens), out_shape=(block, block...]
    dot_general x9 -> x0, matrix products: 14.6 us -> none  [the longest x1 3.66 us: on_device(): jnp.einsum('gqhe,gkthe->ghqkt', grad_heads, value_heads, preferred_elemen...]
    all_gather x1 -> x0, blocking collectives: 11.2 us -> none  [on_device(): upstream = lax.all_gather(grad_output, 'head', axis=1, tiled=True)]
    ppermute x30 -> x0, waiting for transfers between devices: 10.2 us -> none  [shifted(): return lax.ppermute(value, axis, pairs)]
  transfers between devices with their start and end apart: 32 -> 0, of which waited for: 4 -> 0; matrix products, arithmetic and copies ran while one was open for 5% -> 0% of each run, Pallas kernels for 0% -> 0%
where the time goes in v1:
time: 122 us
  Pallas kernels  111 us (91%)
  local copies, waits for them, and re-layouts  10.2 us (8%)
    pallas_call x1, Pallas kernels, on_device(): pl.pallas_call(functools.partial(kernel, tokens), out_shape=(block, block...  111 us
    unnamed x21, local copies, waits for them, and re-layouts  10.2 us

profile of v1, /device:TPU:1, one launch (start us, length us, event | category | flops | bytes accessed | tf_op | source)
XLA Modules:
  0.0 122.1 jit_solution(6124405268291675113)
XLA Ops:
  0.6 0.0 copy-start
  0.6 1.0 copy-done
  1.7 0.0 copy-start.1
  1.7 0.9 copy-done.1
  2.6 0.0 copy-start.2
  2.6 0.9 copy-done.2
  3.5 0.0 copy-start.3
  3.5 0.9 copy-done.3
  4.4 0.0 copy-start.4
  4.4 0.9 copy-done.4
  5.3 0.0 copy-start.5
  5.3 0.7 copy-done.5
  6.0 0.0 copy-start.6
  6.0 0.7 copy-done.6
  6.6 0.0 copy-start.7
  6.6 0.7 copy-done.7
  7.3 111.2 %shard_map.119 = (bf16[256,256]{1,0:T(8,128)(2,1)S(1)}, bf16[256,256]{1,0:T(8,128)(2,1)S(1)}, bf16[256,256]{1,0:T(8,128)(2,1)S(1)}, bf16[256,256]{1,0:T(8,128)(2,1)S(1)}, f32[256,1024]{1,0:T(8,128)S(1)}) custom-call(bf16[256,256]{1,0:T(8,128)(2,1)S(1)} %copy-done.1, bf16[256,256]{1,0:T(8,128)(2,1)S(1)} %copy-done.2, bf16[256,256]{1,0:T(8,128)(2,1)S(1)} %copy-done.3, ...), custom_call_target="tpu_custom_call" | custom-call | tf_op jit(solution)/shard_map/pallas_call | solution.py:503
  118.5 0.7 copy.18
  119.1 0.7 copy.19
  119.8 0.7 copy.20
  120.5 0.7 copy.21
  121.1 1.0 copy.22
Async XLA Ops:
  0.6 1.0 copy-start
  1.7 0.9 copy-start.1
  2.6 0.9 copy-start.2
  3.5 0.9 copy-start.3
  4.4 0.9 copy-start.4
  5.3 0.7 copy-start.5
  6.0 0.7 copy-start.6
  6.6 0.7 copy-start.7

commit v2 on v1

v2 whole, which is shorter than its diff:
```python
import functools
import math

import jax
import jax.numpy as jnp
from jax import lax
from jax.experimental import pallas as pl
from jax.experimental.pallas import tpu as pltpu
from jax.sharding import PartitionSpec as P

HEAD_DIM = 64
BLOCK = 128
HEADS = 4
FEAT = 256
TOK = 256
SLOTS = 8
NEG = -1e30
F32 = jnp.float32
BF16 = jnp.bfloat16
SCALE = HEAD_DIM**-0.5
SCALE2 = SCALE * math.log2(math.e)
MESH = pl.DeviceIdType.MESH

STEPS = ((2, 2), (-2, -2), (1, -1), (3, 1), (-1, -3), (-3, 3))
SLOT_X = (1, -1, 0, 1, -1, 2)


def link_of(step):
    return step - 1 if step > 0 else 2 - step


def nt(a, b):
    return lax.dot_general(a, b, (((1,), (1,)), ((), ())), preferred_element_type=F32)


def nn(a, b):
    return jnp.dot(a, b, preferred_element_type=F32)


def kernel(
    tokens,
    q_ref,
    k_ref,
    v_ref,
    go_ref,
    w_ref,
    link_ref,
    cloud_ref,
    edge_ref,
    out_ref,
    dq_ref,
    dk_ref,
    dv_ref,
    dw_ref,
    w_in,
    kv,
    qg,
    meta,
    stat,
    dof,
    wc,
    at,
    qb,
    gb,
    bias,
    nkv,
    s_buf,
    p_buf,
    low_buf,
    mcol,
    rcol,
    dcol,
    dk_acc,
    dv_acc,
    dwp,
    cs,
    cr,
    xs,
    xr,
    xf,
    zs,
    gx,
    gc,
    send,
    recv,
    local,
):
    strip = lax.axis_index("strip")
    y = lax.axis_index("head")
    core = strip % 2
    z = (strip // 2) % 16
    x = strip // 32
    upper = z // 8

    def at_chip(dx, dz, other=0):
        c = (core + other) % 2
        return (((x + dx + 4) % 4) * 32 + ((z + dz) % 16) * 2 + c, y)

    quad = z // 4

    def near(n):
        return (((x + n // 4) % 4) * 32 + (quad * 4 + (z + n % 4) % 4) * 2 + core, y)

    def near_piece(n):
        return (x + n // 4) % 4 * 4 + (z + n % 4) % 4

    def at_head(dy):
        return (strip, (y + dy) % 4)

    counter = [0]

    def copy(src, dst, device):
        i = counter[0]
        counter[0] += 1
        made = pltpu.make_async_remote_copy(
            src_ref=src,
            dst_ref=dst,
            send_sem=send.at[i],
            recv_sem=recv.at[i],
            device_id=device,
            device_id_type=MESH,
        )
        return made

    peers = [near(n) for n in range(1, 16)]
    peers += [at_chip(0, dz) for dz in (4, 8, 12)]
    peers += [at_chip(dx, 8) for dx in (1, 2, 3)]
    peers += [at_head(dy) for dy in (1, 2, 3)]
    peers += [at_chip(0, 0, 1)]
    barrier = pltpu.get_barrier_semaphore()
    for peer in peers:
        pl.semaphore_signal(barrier, inc=1, device_id=peer, device_id_type=MESH)

    my_columns = pl.ds(pl.multiple_of(y * FEAT, FEAT), FEAT)
    pair = pl.ds(6, 2)
    fills = [pltpu.make_async_copy(go_ref, dof.at[y], local.at[0])]
    fills += [pltpu.make_async_copy(w_ref, w_in, local.at[1])]
    fills += [pltpu.make_async_copy(w_ref.at[:, my_columns], wc.at[y], local.at[2])]
    for g in range(2):
        fills += [pltpu.make_async_copy(q_ref, qg.at[0, g, pair], local.at[3 + g])]
        fills += [pltpu.make_async_copy(k_ref, kv.at[0, g, pair], local.at[5 + g])]
        fills += [pltpu.make_async_copy(v_ref, kv.at[1, g, pair], local.at[7 + g])]
    for made in fills:
        made.start()

    row_id = lax.broadcasted_iota(jnp.int32, (16, BLOCK), 0)
    mine = jnp.zeros((16, BLOCK), jnp.int32)
    member = []
    for g in range(2):
        live = jnp.where(cloud_ref[g] == 0, edge_ref[g], 0)
        mine = jnp.where(row_id == g, live, mine)
        row = []
        for l in range(6):
            has = jnp.int32(0)
            for n in range(4):
                has = has + jnp.where(link_ref[g, n] == l, 1, 0)
            row.append(has)
            mine = jnp.where(row_id == 2 + 6 * g + l, has, mine)
        member.append(row)
    meta[6] = mine

    pl.semaphore_wait(barrier, len(peers))

    own_grad = qg.at[1, 0, pair]
    sources = (k_ref, v_ref, q_ref, own_grad)
    places = [kv.at[0], kv.at[1], qg.at[0], qg.at[1]]
    cross, own, onward = [], [], []
    for src, place in zip(sources, places):
        cross.append([[copy(src.at[g], place.at[g, 2], at_chip(0, 8))] for g in range(2)])
        own.append(
            [copy(src, place.at[:, 1], at_chip(1, 0)), copy(src, place.at[:, 0], at_chip(-1, 0))]
        )
        onward.append(
            [
                [
                    copy(place.at[g, 2], place.at[g, 4], at_chip(1, 0)),
                    copy(place.at[g, 2], place.at[g, 3], at_chip(-1, 0)),
                    copy(place.at[g, 2], place.at[g, 5], at_chip(2, 0)),
                ]
                for g in range(2)
            ]
        )

    def to_far(buf):
        return [
            copy(buf.at[6], buf.at[1], at_chip(1, 0)),
            copy(buf.at[6], buf.at[0], at_chip(-1, 0)),
            copy(buf.at[6], buf.at[2], at_chip(0, 8)),
            copy(buf.at[6], buf.at[4], at_chip(1, 8)),
            copy(buf.at[6], buf.at[3], at_chip(-1, 8)),
            copy(buf.at[6], buf.at[5], at_chip(2, 8)),
        ]

    meta_out = to_far(meta)
    stat_out = to_far(stat)
    y_go = [copy(go_ref, dof.at[y], at_head(dy)) for dy in (1, 2, 3)]
    y_w = [
        copy(
            w_ref.at[:, pl.ds(pl.multiple_of((y + dy) % 4 * FEAT, FEAT), FEAT)],
            wc.at[y],
            at_head(dy),
        )
        for dy in (1, 2, 3)
    ]
    y_at = [copy(at.at[y], at.at[y], at_head(dy)) for dy in (1, 2, 3)]
    c_rs = copy(cs, cr, at_chip(0, 0, 1))
    z_sum = [copy(zs.at[quad], zs.at[quad], at_chip(0, dz)) for dz in (4, 8, 12)]
    c_ag = copy(gx, gc, at_chip(0, 0, 1))
    base = counter[0]

    def near_rs(n):
        return pltpu.make_async_remote_copy(
            src_ref=xs.at[near_piece(n)],
            dst_ref=xr.at[n],
            send_sem=send.at[base + n],
            recv_sem=recv.at[base + n],
            device_id=near(n),
            device_id_type=MESH,
        )

    def near_ag(n):
        return pltpu.make_async_remote_copy(
            src_ref=gx.at[near_piece(0)],
            dst_ref=gx.at[near_piece(0)],
            send_sem=send.at[base + 16 + n],
            recv_sem=recv.at[base + 16 + n],
            device_id=near(n),
            device_id_type=MESH,
        )

    def start(copies):
        for made in copies:
            made.start()

    def arrived(copies):
        for made in copies:
            made.wait_recv()

    def sent(copies):
        for made in copies:
            made.wait_send()

    key, value, query, cot = range(4)
    for g in range(2):
        start(cross[key][g])
    for g in range(2):
        start(cross[value][g])
    start(y_go)
    start(meta_out)

    head_of = lax.broadcasted_iota(jnp.int32, (1, FEAT), 1) // HEAD_DIM
    in_head = [jnp.where(head_of == h, 1.0, 0.0).astype(F32) for h in range(HEADS)]
    in_head_low = [m.astype(BF16) for m in in_head]

    def spread(block):
        return jnp.concatenate([block * m for m in in_head_low], axis=0)

    def gathered(full):
        total = full[:BLOCK] * in_head[0]
        for h in range(1, HEADS):
            total = total + full[h * BLOCK : (h + 1) * BLOCK] * in_head[h]
        return total

    for made in fills:
        made.wait()
    for g in range(2):
        qb[g] = spread(qg[0, 0, 6 + g])

    arrived(y_go)
    grad = nt(dof[0], w_in[:, :FEAT])
    for i in range(1, 4):
        grad = grad + nt(dof[i], w_in[:, i * FEAT : (i + 1) * FEAT])
    grad = grad.astype(BF16)
    for g in range(2):
        for b in range(2):
            qg[1, g, 6 + b] = grad[b * BLOCK : (b + 1) * BLOCK]
        gb[g] = spread(grad[g * BLOCK : (g + 1) * BLOCK])
    start(own[key])
    start(own[value])

    def pass_on(t, g):
        arrived(cross[t][g])
        start(onward[t][g])

    for g in range(2):
        pass_on(key, g)
    for g in range(2):
        start(cross[query][g])

    arrived(meta_out)
    lane = lax.broadcasted_iota(jnp.int32, (1, BLOCK), 1)
    chain = 2 * x + upper
    for g in range(2):
        own_live = jnp.where(cloud_ref[g] == 0, edge_ref[g], 0)
        for j in range(6):
            far = meta[j]
            low_step, high_step = STEPS[j]
            step = jnp.where(upper == 0, low_step, high_step)
            inside = jnp.where((chain + step >= 0) & (chain + step < 8), 1, 0)
            listed = inside * jnp.where(
                upper == 0, member[g][link_of(low_step)], member[g][link_of(high_step)]
            )
            live = far[g : g + 1] * listed
            bias[g, :, j * BLOCK : (j + 1) * BLOCK] = jnp.where(lane < live, 0.0, NEG).astype(F32)
            here_low = 2 + 6 * g + link_of(-low_step)
            here_high = 2 + 6 * g + link_of(-high_step)
            lists_us = jnp.where(
                upper == 0, far[here_low : here_low + 1], far[here_high : here_high + 1]
            )
            nkv[g, j] = lists_us * (inside * own_live)
        for b in range(2):
            live = edge_ref[b] if b == g else jnp.where(cloud_ref[b] == 0, edge_ref[b], 0)
            bias[g, :, (6 + b) * BLOCK : (7 + b) * BLOCK] = jnp.where(lane < live, 0.0, NEG).astype(F32)
            nkv[b, 6 + g] = jnp.full((1, BLOCK), live, jnp.int32)

    CHUNK = 32

    def scores(g):
        keys = kv[0, g].reshape(SLOTS * BLOCK, FEAT)
        s_buf[...] = nt(qb[g], keys)

        def soft(r, _):
            rows = pl.ds(pl.multiple_of(r * CHUNK, CHUNK), CHUNK)
            s = s_buf[rows, :] * SCALE2 + bias[g]
            top = jnp.max(s, axis=1, keepdims=True)
            e = jnp.exp2(s - top)
            inv = 1.0 / jnp.sum(e, axis=1, keepdims=True)
            p = e * inv
            p_buf[g, rows, :] = p
            low_buf[g, rows, :] = p.astype(BF16)
            mcol[g, rows, :] = jnp.broadcast_to(top, (CHUNK, BLOCK))
            rcol[g, rows, :] = jnp.broadcast_to(inv, (CHUNK, BLOCK))
            return 0

        lax.fori_loop(0, HEADS * BLOCK // CHUNK, soft, 0)

    def values(g):
        full = nn(low_buf[g], kv[1, g].reshape(SLOTS * BLOCK, FEAT))
        at[y, g * BLOCK : (g + 1) * BLOCK, :] = gathered(full).astype(BF16)

    pass_on(value, 0)
    for g in range(2):
        start(cross[cot][g])
    pass_on(value, 1)
    start(y_w)
    start(own[query])
    start(own[cot])
    arrived(own[key])
    for g in range(2):
        arrived(onward[key][g])
        scores(g)
    arrived(own[value])
    for g in range(2):
        arrived(onward[value][g])
        values(g)

    start(y_at)
    attn_t = at[y].astype(F32).T.astype(BF16)
    weight_scale = tokens ** (-0.5)
    for i in range(4):
        dwp[i] = nn(attn_t, dof[i]) * weight_scale
    theirs = pl.ds(pl.multiple_of((1 - core) * BLOCK, BLOCK), BLOCK)
    ours = pl.ds(pl.multiple_of(core * BLOCK, BLOCK), BLOCK)
    for i in range(4):
        cs[i] = dwp[i, theirs, :].astype(BF16)
    c_rs.start()

    lane_full = lax.broadcasted_iota(jnp.int32, (BLOCK, BLOCK), 1)

    def correction(g):
        t = qg[1, g, 6 + g].astype(F32) * at[y, g * BLOCK : (g + 1) * BLOCK, :].astype(F32)
        packed = jnp.zeros((BLOCK, BLOCK), F32)
        for h in range(HEADS):
            rows = slice(h * BLOCK, (h + 1) * BLOCK)
            d = jnp.broadcast_to(jnp.sum(t * in_head[h], axis=1, keepdims=True), (BLOCK, BLOCK))
            dcol[g, rows, :] = d
            packed = jnp.where(lane_full == h, mcol[g, rows, :], packed)
            packed = jnp.where(lane_full == HEADS + h, rcol[g, rows, :], packed)
            packed = jnp.where(lane_full == 2 * HEADS + h, d, packed)
        stat[6, g] = packed.T[:16]

    def backward_queries(g):
        keys = kv[0, g].reshape(SLOTS * BLOCK, FEAT)
        s_buf[...] = nt(gb[g], kv[1, g].reshape(SLOTS * BLOCK, FEAT))

        def body(r, _):
            rows = pl.ds(pl.multiple_of(r * CHUNK, CHUNK), CHUNK)
            ds = p_buf[g, rows, :] * (s_buf[rows, :] - dcol[g, rows, 0:1])
            low_buf[g, rows, :] = ds.astype(BF16)
            return 0

        lax.fori_loop(0, HEADS * BLOCK // CHUNK, body, 0)
        full = nn(low_buf[g], keys)
        dq_ref[g] = (gathered(full) * SCALE).astype(BF16)

    row_full = lax.broadcasted_iota(jnp.int32, (BLOCK, BLOCK), 0)

    def keys_step(g, j, slot, group):
        queries, cots = spread(qg[0, g, j]), spread(qg[1, g, j])
        st = nt(kv[0, g, 6 + g], queries)
        dp = nt(kv[1, g, 6 + g], cots)
        off = jnp.where(row_full < nkv[g, j], 0.0, NEG).astype(F32)
        rows = stat[slot, group]
        lows, ds = [], []
        for h in range(HEADS):
            cols = slice(h * BLOCK, (h + 1) * BLOCK)
            top = rows[h : h + 1]
            inv = rows[HEADS + h : HEADS + h + 1]
            d = rows[2 * HEADS + h : 2 * HEADS + h + 1]
            p = jnp.exp2(st[:, cols] * SCALE2 + off - top) * inv
            lows.append(p.astype(BF16))
            ds.append((p * (dp[:, cols] - d)).astype(BF16))
        dv_acc[g] += nn(jnp.concatenate(lows, axis=1), cots)
        dk_acc[g] += nn(jnp.concatenate(ds, axis=1), queries)

    def keys_near(g):
        dv_acc[g] = jnp.zeros((BLOCK, FEAT), F32)
        dk_acc[g] = jnp.zeros((BLOCK, FEAT), F32)

        def body(b, _):
            keys_step(g, 6 + b, 6, b)
            return 0

        lax.fori_loop(0, 2, body, 0)

    def keys_far(g, first, last):
        def body(j, _):
            keys_step(g, j, j, g)
            return 0

        lax.fori_loop(first, last, body, 0)

    def each_near(act):
        def body(n, _):
            act(n)
            return 0

        lax.fori_loop(1, 16, body, 0)

    correction(0)
    correction(1)
    start(stat_out)
    c_rs.wait_recv()
    for i in range(4):
        part = dwp[i, ours, :] + cr[i].astype(F32)
        for r in range(4):
            piece = part[r * 32 : (r + 1) * 32]
            xf[4 * i + r] = piece
            xs[4 * i + r] = piece.astype(BF16)
    each_near(lambda n: near_rs(n).start())
    for g in range(2):
        pass_on(query, g)
    backward_queries(0)

    each_near(lambda n: near_rs(n).wait_recv())
    part = xf[near_piece(0)]
    for n in range(1, 16):
        part = part + xr[n].astype(F32)
    zs[quad] = part.astype(BF16)
    start(z_sum)
    for g in range(2):
        pass_on(cot, g)
    backward_queries(1)

    arrived(y_at)
    arrived(y_w)
    result = nn(at[0], wc[0])
    for i in range(1, 4):
        result = result + nn(at[i], wc[i])
    for b in range(2):
        out_ref[b] = result[b * BLOCK : (b + 1) * BLOCK].astype(BF16)

    arrived(z_sum)
    part = zs[0].astype(F32)
    for i in range(1, 4):
        part = part + zs[i].astype(F32)
    gx[near_piece(0)] = part.astype(BF16)
    each_near(lambda n: near_ag(n).start())

    for g in range(2):
        keys_near(g)
    arrived(stat_out)
    arrived(own[query])
    arrived(own[cot])
    for g in range(2):
        keys_far(g, 0, 2)
    each_near(lambda n: near_ag(n).wait_recv())
    c_ag.start()
    for g in range(2):
        arrived(onward[query][g])
        arrived(onward[cot][g])
        keys_far(g, 2, 6)
        dk_ref[g] = (dk_acc[g] * SCALE).astype(BF16)
        dv_ref[g] = dv_acc[g].astype(BF16)

    def assemble(buf, first_row):
        for i in range(4):
            for r in range(4):
                rows = pl.ds(pl.multiple_of(first_row + r * 32, 32), 32)
                dw_ref[rows, i * FEAT : (i + 1) * FEAT] = buf[4 * i + r].astype(F32)

    assemble(gx, core * BLOCK)
    c_ag.wait_recv()
    assemble(gc, (1 - core) * BLOCK)

    for t in range(4):
        for g in range(2):
            sent(cross[t][g])
            sent(onward[t][g])
        sent(own[t])
    for copies in (meta_out, stat_out, y_go, y_w, y_at, z_sum):
        sent(copies)
    c_rs.wait_send()
    c_ag.wait_send()
    each_near(lambda n: near_rs(n).wait_send())
    each_near(lambda n: near_ag(n).wait_send())


SEMAPHORES = 128


def on_device(
    queries, keys_in, values_in, grad_output, w_output, link_dilation_index, clouds, edge_lengths
):
    tokens = queries.shape[0] * lax.axis_size("strip")
    vmem = pl.BlockSpec(memory_space=pltpu.VMEM)
    smem = pl.BlockSpec(memory_space=pltpu.SMEM)
    shape = (2, BLOCK, FEAT)
    block = jax.ShapeDtypeStruct(shape, BF16)
    anywhere = pl.BlockSpec(memory_space=pl.ANY)
    result, dq, dk, dv, dw = pl.pallas_call(
        functools.partial(kernel, tokens),
        out_shape=(block, block, block, block, jax.ShapeDtypeStruct((FEAT, 4 * FEAT), F32)),
        in_specs=[anywhere] * 5 + [smem] * 3,
        out_specs=(vmem,) * 5,
        scratch_shapes=[
            pltpu.VMEM((FEAT, 4 * FEAT), BF16),
            pltpu.VMEM((2, 2, SLOTS, BLOCK, FEAT), BF16),
            pltpu.VMEM((2, 2, SLOTS, BLOCK, FEAT), BF16),
            pltpu.VMEM((7, 16, BLOCK), jnp.int32),
            pltpu.VMEM((7, 2, 16, BLOCK), F32),
            pltpu.VMEM((4, TOK, FEAT), BF16),
            pltpu.VMEM((4, FEAT, FEAT), BF16),
            pltpu.VMEM((4, TOK, FEAT), BF16),
            pltpu.VMEM((2, HEADS * BLOCK, FEAT), BF16),
            pltpu.VMEM((2, HEADS * BLOCK, FEAT), BF16),
            pltpu.VMEM((2, 1, SLOTS * BLOCK), F32),
            pltpu.VMEM((2, SLOTS, 1, BLOCK), jnp.int32),
            pltpu.VMEM((HEADS * BLOCK, SLOTS * BLOCK), F32),
            pltpu.VMEM((2, HEADS * BLOCK, SLOTS * BLOCK), F32),
            pltpu.VMEM((2, HEADS * BLOCK, SLOTS * BLOCK), BF16),
            pltpu.VMEM((2, HEADS * BLOCK, BLOCK), F32),
            pltpu.VMEM((2, HEADS * BLOCK, BLOCK), F32),
            pltpu.VMEM((2, HEADS * BLOCK, BLOCK), F32),
            pltpu.VMEM((2, BLOCK, FEAT), F32),
            pltpu.VMEM((2, BLOCK, FEAT), F32),
            pltpu.VMEM((4, FEAT, FEAT), F32),
            pltpu.VMEM((4, BLOCK, FEAT), BF16),
            pltpu.VMEM((4, BLOCK, FEAT), BF16),
            pltpu.VMEM((16, 32, FEAT), BF16),
            pltpu.VMEM((16, 32, FEAT), BF16),
            pltpu.VMEM((16, 32, FEAT), F32),
            pltpu.VMEM((4, 32, FEAT), BF16),
            pltpu.VMEM((16, 32, FEAT), BF16),
            pltpu.VMEM((16, 32, FEAT), BF16),
            pltpu.SemaphoreType.DMA((SEMAPHORES,)),
            pltpu.SemaphoreType.DMA((SEMAPHORES,)),
            pltpu.SemaphoreType.DMA((9,)),
        ],
        compiler_params=pltpu.CompilerParams(
            collective_id=0, has_side_effects=True, vmem_limit_bytes=60 * 2**20
        ),
    )(
        queries.reshape(shape),
        keys_in.reshape(shape),
        values_in.reshape(shape),
        grad_output,
        w_output,
        link_dilation_index,
        clouds,
        edge_lengths,
    )
    flat = (TOK, FEAT)
    return result.reshape(flat), dq.reshape(flat), dk.reshape(flat), dv.reshape(flat), dw


def solution(mesh):
    return jax.shard_map(
        on_device,
        mesh=mesh,
        in_specs=(
            P("strip", "head"),
            P("strip", "head"),
            P("strip", "head"),
            P("strip", "head"),
            P("head", None),
            P("strip", None),
            P("strip"),
            P("strip"),
        ),
        out_specs=(
            P("strip", "head"),
            P("strip", "head"),
            P("strip", "head"),
            P("strip", "head"),
            P("head", None),
        ),
        check_vma=False,
    )
```

time: 122 us -> 111 us (0.910); the launches traced: 122 us -> 110 us
  Pallas kernels: 111 us -> 102 us
  local copies, waits for them, and re-layouts: 10.2 us -> 7.33 us
    pallas_call x1, Pallas kernels: 111 us -> 102 us  [on_device(): pl.pallas_call(functools.partial(kernel, tokens), out_shape=(block, block...]
    unnamed x21 -> x7, local copies, waits for them, and re-layouts: 10.2 us -> 7.33 us
where the time goes in v2:
time: 111 us; the launch traced here: 110 us
  Pallas kernels  102 us (92%)
  local copies, waits for them, and re-layouts  7.33 us (7%)
    pallas_call x1, Pallas kernels, on_device(): pl.pallas_call(functools.partial(kernel, tokens), out_shape=(block, block...  102 us
    unnamed x7, local copies, waits for them, and re-layouts  7.33 us

profile of v2, /device:TPU:1, one launch (start us, length us, event | category | flops | bytes accessed | tf_op | source)
XLA Modules:
  0.0 109.8 jit_solution(6691390001759752375)
XLA Ops:
  0.6 101.8 %shard_map.119 = (bf16[2,128,256]{2,1,0:T(8,128)(2,1)}, bf16[2,128,256]{2,1,0:T(8,128)(2,1)}, bf16[2,128,256]{2,1,0:T(8,128)(2,1)}, bf16[2,128,256]{2,1,0:T(8,128)(2,1)}, f32[256,1024]{1,0:T(8,128)}) custom-call(bf16[2,128,256]{2,1,0:T(8,128)(2,1)} %bitcast.11, bf16[2,128,256]{2,1,0:T(8,128)(2,1)} %bitcast.12, bf16[2,128,256]{2,1,0:T(8,128)(2,1)} %bitcast.13, ...), custom_call_target="tpu_custom_call" | custom-call | tf_op jit(solution)/shard_map/pallas_call | solution.py:531
  102.4 0.0 copy-start
  102.5 1.7 %copy.18 = bf16[256,256]{1,0:T(8,128)(2,1)} copy(bf16[256,256]{1,0:T(8,128)(2,1)} %bitcast.10) | data formatting | bytes 262144
  104.1 1.6 %copy.19 = bf16[256,256]{1,0:T(8,128)(2,1)} copy(bf16[256,256]{1,0:T(8,128)(2,1)} %bitcast.9) | data formatting | bytes 262144
  105.7 1.6 %copy.20 = bf16[256,256]{1,0:T(8,128)(2,1)} copy(bf16[256,256]{1,0:T(8,128)(2,1)} %bitcast.8) | data formatting | bytes 262144
  107.2 1.6 %copy.21 = bf16[256,256]{1,0:T(8,128)(2,1)} copy(bf16[256,256]{1,0:T(8,128)(2,1)} %bitcast.7) | data formatting | bytes 262144
  108.8 0.0 copy-done
  108.8 1.0 copy.22
Async XLA Ops:
  102.4 6.4 %copy-start = (f32[256,1024]{1,0:T(8,128)S(1)}, f32[256,1024]{1,0:T(8,128)}, u32[]{:S(2)}) copy-start(f32[256,1024]{1,0:T(8,128)} %get-tuple-element.24) | copy-start | bytes 3145732

commit v3 on v2

--- a/solution.py
+++ b/solution.py
@@ -205,7 +205,10 @@
     y_at = [copy(at.at[y], at.at[y], at_head(dy)) for dy in (1, 2, 3)]
     c_rs = copy(cs, cr, at_chip(0, 0, 1))
     z_sum = [copy(zs.at[quad], zs.at[quad], at_chip(0, dz)) for dz in (4, 8, 12)]
-    c_ag = copy(gx, gc, at_chip(0, 0, 1))
+    def quarter(dx):
+        return pl.ds((x - dx + 4) % 4 * 4, 4)
+
+    c_ag = [copy(gx.at[quarter(dx)], gc.at[quarter(dx)], at_chip(0, 0, 1)) for dx in range(4)]
     base = counter[0]
 
     def near_rs(n):
@@ -484,12 +487,18 @@
     arrived(own[cot])
     for g in range(2):
         keys_far(g, 0, 2)
-    each_near(lambda n: near_ag(n).wait_recv())
-    c_ag.start()
-    for g in range(2):
-        arrived(onward[query][g])
-        arrived(onward[cot][g])
-        keys_far(g, 2, 6)
+    arrived(onward[query][0])
+    arrived(onward[cot][0])
+    keys_far(0, 2, 6)
+    for dx in range(4):
+        for n in range(max(1, 4 * dx), 4 * dx + 4):
+            near_ag(n).wait_recv()
+        c_ag[dx].start()
+    for g in range(2):
+        if g == 1:
+            arrived(onward[query][g])
+            arrived(onward[cot][g])
+            keys_far(g, 2, 6)
         dk_ref[g] = (dk_acc[g] * SCALE).astype(BF16)
         dv_ref[g] = dv_acc[g].astype(BF16)
 
@@ -500,7 +509,7 @@
                 dw_ref[rows, i * FEAT : (i + 1) * FEAT] = buf[4 * i + r].astype(F32)
 
     assemble(gx, core * BLOCK)
-    c_ag.wait_recv()
+    arrived(c_ag)
     assemble(gc, (1 - core) * BLOCK)
 
     for t in range(4):
@@ -511,12 +520,17 @@
     for copies in (meta_out, stat_out, y_go, y_w, y_at, z_sum):
         sent(copies)
     c_rs.wait_send()
-    c_ag.wait_send()
+    sent(c_ag)
     each_near(lambda n: near_rs(n).wait_send())
     each_near(lambda n: near_ag(n).wait_send())
 
 
 SEMAPHORES = 128
+
+
+def hand_over(*refs):
+    for src, dst in zip(refs[:5], refs[5:]):
+        dst[...] = src[...]
 
 
 def on_device(
@@ -528,7 +542,7 @@
     shape = (2, BLOCK, FEAT)
     block = jax.ShapeDtypeStruct(shape, BF16)
     anywhere = pl.BlockSpec(memory_space=pl.ANY)
-    result, dq, dk, dv, dw = pl.pallas_call(
+    parts = pl.pallas_call(
         functools.partial(kernel, tokens),
         out_shape=(block, block, block, block, jax.ShapeDtypeStruct((FEAT, 4 * FEAT), F32)),
         in_specs=[anywhere] * 5 + [smem] * 3,
@@ -580,6 +594,12 @@
         clouds,
         edge_lengths,
     )
+    result, dq, dk, dv, dw = pl.pallas_call(
+        hand_over,
+        out_shape=[jax.ShapeDtypeStruct(part.shape, part.dtype) for part in parts],
+        in_specs=[vmem] * 5,
+        out_specs=[vmem] * 5,
+    )(*parts)
     flat = (TOK, FEAT)
     return result.reshape(flat), dq.reshape(flat), dk.reshape(flat), dv.reshape(flat), dw
 

time: 111 us -> 105 us (0.946)
  local copies, waits for them, and re-layouts: 7.33 us -> 0 us
  Pallas kernels: 102 us -> 104 us
    unnamed x7 -> x0, local copies, waits for them, and re-layouts: 7.33 us -> none
    pallas_call x0 -> x1, Pallas kernels: none -> 2.65 us  [on_device(): pl.pallas_call(hand_over, out_shape=[jax.ShapeDtypeStruct(part.shape, par...]
where the time goes in v3:
time: 105 us
  Pallas kernels  104 us (99%)
    pallas_call x1, Pallas kernels, on_device(): pl.pallas_call(functools.partial(kernel, tokens), out_shape=(block, block...  101 us
    pallas_call x1, Pallas kernels, on_device(): pl.pallas_call(hand_over, out_shape=[jax.ShapeDtypeStruct(part.shape, par...  2.65 us

profile of v3, /device:TPU:1, one launch (start us, length us, event | category | flops | bytes accessed | tf_op | source)
XLA Modules:
  0.0 104.6 jit_solution(6386085978176009280)
XLA Ops:
  0.6 101.3 %shard_map.119 = (bf16[2,128,256]{2,1,0:T(8,128)(2,1)}, bf16[2,128,256]{2,1,0:T(8,128)(2,1)}, bf16[2,128,256]{2,1,0:T(8,128)(2,1)}, bf16[2,128,256]{2,1,0:T(8,128)(2,1)}, f32[256,1024]{1,0:T(8,128)}) custom-call(bf16[2,128,256]{2,1,0:T(8,128)(2,1)} %bitcast.7, bf16[2,128,256]{2,1,0:T(8,128)(2,1)} %bitcast.8, bf16[2,128,256]{2,1,0:T(8,128)(2,1)} %bitcast.9, ...), custom_call_target="tpu_custom_call" | custom-call | tf_op jit(solution)/shard_map/pallas_call | solution.py:545
  102.0 2.6 %shard_map.120 = (bf16[2,128,256]{2,1,0:T(8,128)(2,1)}, bf16[2,128,256]{2,1,0:T(8,128)(2,1)}, bf16[2,128,256]{2,1,0:T(8,128)(2,1)}, bf16[2,128,256]{2,1,0:T(8,128)(2,1)}, f32[256,1024]{1,0:T(8,128)}) custom-call(bf16[2,128,256]{2,1,0:T(8,128)(2,1)} %get-tuple-element.15.refs_0_, bf16[2,128,256]{2,1,0:T(8,128)(2,1)} %get-tuple-element.16.refs_1_, ...), custom_call_target="tpu_custom_call" | custom-call | tf_op jit(solution)/shard_map/pallas_call | solution.py:597

commit v4 on v3

--- a/solution.py
+++ b/solution.py
@@ -487,20 +487,17 @@
     arrived(own[cot])
     for g in range(2):
         keys_far(g, 0, 2)
-    arrived(onward[query][0])
-    arrived(onward[cot][0])
-    keys_far(0, 2, 6)
+    for g in range(2):
+        arrived(onward[query][g])
+        arrived(onward[cot][g])
+        keys_far(g, 2, 6)
+        dk_ref[g] = (dk_acc[g] * SCALE).astype(BF16)
+        dv_ref[g] = dv_acc[g].astype(BF16)
+
     for dx in range(4):
         for n in range(max(1, 4 * dx), 4 * dx + 4):
             near_ag(n).wait_recv()
         c_ag[dx].start()
-    for g in range(2):
-        if g == 1:
-            arrived(onward[query][g])
-            arrived(onward[cot][g])
-            keys_far(g, 2, 6)
-        dk_ref[g] = (dk_acc[g] * SCALE).astype(BF16)
-        dv_ref[g] = dv_acc[g].astype(BF16)
 
     def assemble(buf, first_row):
         for i in range(4):

time: 105 us -> 105 us (level)
  no operation moved by 1% of the time
where the time goes in v4:
time: 105 us
  Pallas kernels  104 us (99%)
    pallas_call x1, Pallas kernels, on_device(): pl.pallas_call(functools.partial(kernel, tokens), out_shape=(block, block...  101 us
    pallas_call x1, Pallas kernels, on_device(): pl.pallas_call(hand_over, out_shape=[jax.ShapeDtypeStruct(part.shape, par...  2.65 us

profile of v4, /device:TPU:1, one launch (start us, length us, event | category | flops | bytes accessed | tf_op | source)
XLA Modules:
  0.0 104.6 jit_solution(15648808363772760744)
XLA Ops:
  0.6 101.3 %shard_map.119 = (bf16[2,128,256]{2,1,0:T(8,128)(2,1)}, bf16[2,128,256]{2,1,0:T(8,128)(2,1)}, bf16[2,128,256]{2,1,0:T(8,128)(2,1)}, bf16[2,128,256]{2,1,0:T(8,128)(2,1)}, f32[256,1024]{1,0:T(8,128)}) custom-call(bf16[2,128,256]{2,1,0:T(8,128)(2,1)} %bitcast.7, bf16[2,128,256]{2,1,0:T(8,128)(2,1)} %bitcast.8, bf16[2,128,256]{2,1,0:T(8,128)(2,1)} %bitcast.9, ...), custom_call_target="tpu_custom_call" | custom-call | tf_op jit(solution)/shard_map/pallas_call | solution.py:542
  102.0 2.6 %shard_map.120 = (bf16[2,128,256]{2,1,0:T(8,128)(2,1)}, bf16[2,128,256]{2,1,0:T(8,128)(2,1)}, bf16[2,128,256]{2,1,0:T(8,128)(2,1)}, bf16[2,128,256]{2,1,0:T(8,128)(2,1)}, f32[256,1024]{1,0:T(8,128)}) custom-call(bf16[2,128,256]{2,1,0:T(8,128)(2,1)} %get-tuple-element.15.refs_0_, bf16[2,128,256]{2,1,0:T(8,128)(2,1)} %get-tuple-element.16.refs_1_, ...), custom_call_target="tpu_custom_call" | custom-call | tf_op jit(solution)/shard_map/pallas_call | solution.py:594
